TPU v7x, 32 devices: a whole 2x2x4 slice. The times are simulated.
32 devices in a mesh: ckpt: 8 (over y, x, core), lat: 4 (over z).
Axes of the slice: x: 2, y: 2, z: 4, core: 2. Of those that a mesh axis runs over, the one named last changes fastest.
Arguments:
- hidden_in: bfloat16 [16, 512, 1024], P('ckpt', None, 'lat'), may hold values from -6 to 6
- ln_gain: float32 [16, 1024], P('ckpt'), may hold values from 0.4 to 1.6
- ln_bias: float32 [16, 1024], P('ckpt'), may hold values from -2.5 to 2.5
- w_in: bfloat16 [16, 1024, 4096], P('ckpt', None, 'lat'), may hold values from -0.1875 to 0.1875
- b_in: float32 [16, 4096], P('ckpt', 'lat'), may hold values from -3 to 3
- w_out: bfloat16 [16, 4096, 1024], P('ckpt', 'lat'), may hold values from -0.09375 to 0.09375
- b_out: float32 [16, 1024], P('ckpt'), may hold values from -3 to 3
- w_enc: bfloat16 [16, 1024, 8192], P('ckpt', None, 'lat'), may hold values from -0.046875 to 0.046875
- b_enc: float32 [8192], P('lat'), may hold values from -3 to 3
- w_dec: bfloat16 [16, 8192, 1024], P('ckpt', 'lat'), may hold values from -6 to 6
- b_dec: float32 [16, 1024], P('ckpt'), may hold values from -3 to 3
Outputs:
- grad_enc: bfloat16 [16, 1024, 8192], P('ckpt', None, 'lat')
- grad_benc: float32 [8192], P('lat')
- grad_dec: bfloat16 [16, 8192, 1024], P('ckpt', 'lat')
All inputs are finite; a program needn't handle non-finite values.
Results may differ from a plain program's by a relative error of at most 0.0075.
Values may be sent and summed in bfloat16 or wider, within the bound.
A program may use at most 128 MiB of HBM per device.

v0:
```python
import math

import jax
import jax.numpy as jnp
from jax import lax
from jax.sharding import PartitionSpec as P

norm_eps = 1e-05
row_eps = 1e-06
sparsity_weight = 0.2


def on_device(hidden_in, ln_gain, ln_bias, w_in, b_in, w_out, b_out, w_enc, b_enc, w_dec, b_dec):
    tokens = hidden_in.shape[1]
    feat_cols = hidden_in.shape[2]
    scale = 1.0 / math.sqrt(tokens)
    lat_index = lax.axis_index("lat")
    whole = lax.all_gather(hidden_in, "lat", axis=2, tiled=True)
    floats = whole.astype(jnp.float32)
    center = floats - jnp.mean(floats, -1, keepdims=True)
    spread = jnp.mean(center * center, -1, keepdims=True)
    normed = (
        center * lax.rsqrt(spread + norm_eps) * ln_gain[:, None, :] + ln_bias[:, None, :]
    ).astype(jnp.bfloat16)
    raised = (
        jnp.einsum("ctd,cdf->ctf", normed, w_in, preferred_element_type=jnp.float32)
        + b_in[:, None, :]
    )
    active = jax.nn.gelu(raised, approximate=False).astype(jnp.bfloat16)
    terms = jnp.einsum("ctf,cfd->ctd", active, w_out, preferred_element_type=jnp.float32)
    share = lax.psum_scatter(terms, "lat", scatter_dimension=2, tiled=True)
    out_bias = lax.dynamic_slice_in_dim(b_out, lat_index * feat_cols, feat_cols, 1)
    piece = (hidden_in.astype(jnp.float32) + share + out_bias[:, None, :]).astype(jnp.bfloat16)
    acts = lax.all_gather(piece, "lat", axis=2, tiled=True)
    wide_dec = w_dec.astype(jnp.float32)
    norms = jnp.sqrt(jnp.sum(wide_dec * wide_dec, 2) + row_eps)
    local_total = jnp.sum(norms, 0)
    rows = acts
    pre_sum, total = lax.psum(
        (jnp.einsum("ctd,cdl->tl", rows, w_enc, preferred_element_type=jnp.float32), local_total),
        "ckpt",
    )
    pre = pre_sum + b_enc[None, :]
    feat = jnp.maximum(pre, 0.0).astype(jnp.bfloat16)
    recon_terms = jnp.einsum("tl,cld->ctd", feat, w_dec, preferred_element_type=jnp.float32)
    recon = lax.psum(recon_terms.astype(jnp.bfloat16), "lat").astype(jnp.float32)
    resid = recon + b_dec[:, None, :] - acts.astype(jnp.float32)
    dres = (resid * scale).astype(jnp.bfloat16)
    sparse_term = sparsity_weight * scale * total
    rows = dres
    dfeat = (
        lax.psum(
            jnp.einsum("ctd,cld->tl", rows, w_dec, preferred_element_type=jnp.float32).astype(
                jnp.bfloat16
            ),
            "ckpt",
        ).astype(jnp.float32)
        + sparse_term[None, :]
    )
    dpre = jnp.where(pre > 0.0, dfeat, 0.0).astype(jnp.bfloat16)
    grad_enc = jnp.einsum("ctd,tl->cdl", acts, dpre, preferred_element_type=jnp.float32).astype(
        jnp.bfloat16
    )
    grad_benc = jnp.sum(dpre.astype(jnp.float32), 0)
    column = jnp.sum(feat.astype(jnp.float32), 0)
    main = jnp.einsum("tl,ctd->cld", feat, dres, preferred_element_type=jnp.float32)
    extra = sparsity_weight * scale * column[None, :, None] * wide_dec / norms[:, :, None]
    grad_dec = (main + extra).astype(jnp.bfloat16)
    return (grad_enc, grad_benc, grad_dec)


def solution(mesh):
    placed = (
        P("ckpt", None, "lat"),
        P("ckpt", None),
        P("ckpt", None),
        P("ckpt", None, "lat"),
        P("ckpt", "lat"),
        P("ckpt", "lat", None),
        P("ckpt", None),
        P("ckpt", None, "lat"),
        P("lat"),
        P("ckpt", "lat", None),
        P("ckpt", None),
    )
    return jax.shard_map(
        on_device,
        mesh=mesh,
        in_specs=placed,
        out_specs=(P("ckpt", None, "lat"), P("lat"), P("ckpt", "lat", None)),
        check_vma=False,
    )
```

profile of v0, /device:TPU:0, one launch (start us, length us, event | category | flops | bytes accessed | tf_op | source)
XLA Modules:
  0.0 484.5 jit_solution(8875853700049935944)
XLA Ops:
  7.3 0.7 all-gather.3.cloned.1.call-update
  8.0 50.6 %all-gather.3.cloned.1.call-done = bf16[2,512,1024]{2,1,0:T(8,128)(2,1)} async-done(((bf16[2,512,256]{2,1,0:T(8,128)(2,1)}), bf16[2,512,1024]{2,1,0:T(8,128)(2,1)}) %all-gather.3.cloned.1.call-update) | async-done | bytes 2097168 | tf_op jit(solution)/shard_map/all_gather | solution.py:18
  58.6 2.1 convert_reduce_fusion
  60.7 2.3 fusion.6
  63.0 6.1 %fusion.66 = (u8[512,1024]{1,0:T(8,128)(4,1)S(1)}, u8[512,1024]{1,0:T(8,128)(4,1)S(1)}, f32[2,512,1024]{2,1,0:T(8,128)S(1)}) fusion(f32[2,1024]{1,0:T(2,128)S(1)} %copy-done.9, bf16[2,1024,1024]{2,1,0:T(8,128)(2,1)} %param.14, bf16[2,512,1024]{2,1,0:T(8,128)(2,1)S(1)} %copy-done.2, f32[2,1024]{1,0:T(2,128)S(1)} %copy-done.7, f32[2,1024]{1,0:T(2,128)S(1)} %copy-done.8, ...), kind=kOutput, calls=%fused_computation.89 | convolution fusion | flops 2167406592 | bytes 11567104 | tf_op jit(solution)/shard_map/ctd,cdf->ctf/dot_general | solution.py:26
  69.2 13.3 %fusion.19 = f32[2,512,1024]{2,1,0:T(8,128)} fusion(bf16[2,1024,1024]{2,1,0:T(8,128)(2,1)S(1)} %copy-done.5, f32[2,512,1024]{2,1,0:T(8,128)S(1)} %get-tuple-element.14, f32[2,1024]{1,0:T(2,128)S(1)} %copy-done.9, u8[512,1024]{1,0:T(8,128)(4,1)S(1)} %get-tuple-element.7, u8[512,1024]{1,0:T(8,128)(4,1)S(1)} %get-tuple-element.6), kind=kOutput, calls=%fused_computation.44 | convolution fusion | flops 2221932544 | bytes 13639680 | tf_op jit(solution)/shard_map/ctf,cfd->ctd/dot_general | solution.py:30
  82.5 75.0 %reduce-scatter.2.cloned.1.call-done = f32[2,512,256]{2,1,0:T(8,128)} async-done(((f32[2,512,1024]{2,1,0:T(8,128)}), f32[2,512,256]{2,1,0:T(8,128)}) %reduce-scatter.2.cloned.1.call-update) | async-done | bytes 1048592 | tf_op jit(solution)/shard_map/reduce_scatter | solution.py:31
  157.6 2.2 add_convert_fusion
  159.9 46.9 %all-gather.5.cloned.1.call-done = bf16[2,512,1024]{2,1,0:T(8,128)(2,1)} async-done(((bf16[2,512,256]{2,1,0:T(8,128)(2,1)}), bf16[2,512,1024]{2,1,0:T(8,128)(2,1)}) %all-gather.5.cloned.1.call-update) | async-done | bytes 2097168 | tf_op jit(solution)/shard_map/all_gather | solution.py:34
  206.7 10.5 %convolution_bitcast_fusion = f32[512,2048]{1,0:T(8,128)} fusion(bf16[2,512,1024]{2,1,0:T(8,128)(2,1)} %all-gather.5.cloned.1.call-done, bf16[2,1024,2048]{2,1,0:T(8,128)(2,1)} %param.18), kind=kOutput, calls=%fused_computation.43 | convolution fusion | flops 4294967296 | bytes 14680064 | tf_op jit(solution)/shard_map/ctd,cdl->tl/dot_general | solution.py:40
  217.3 0.2 all-reduce.6.cloned.1.call-start
  217.5 79.2 %all-reduce.4.cloned.1.call-done = f32[512,2048]{1,0:T(8,128)} async-done(((f32[512,2048]{1,0:T(8,128)}), f32[512,2048]{1,0:T(8,128)}) %all-reduce.4.cloned.1.call-update) | async-done | bytes 4194320 | tf_op jit(solution)/shard_map/psum | solution.py:39
  296.7 2.9 convert_reduce_fusion.1
  299.5 9.1 %convert_bitcast_fusion = bf16[2,512,1024]{2,1,0:T(8,128)(2,1)} fusion(bf16[2,2048,1024]{2,1,0:T(8,128)(2,1)} %param.20, bf16[512,2048]{1,0:T(8,128)(2,1)S(1)} %get-tuple-element.9), kind=kOutput, calls=%fused_computation.51 | convolution fusion | flops 4296015872 | bytes 12582912 | tf_op jit(solution)/shard_map/tl,cld->ctd/dot_general | solution.py:45
  308.8 11.6 %copy.14 = bf16[2,2048,1024]{1,2,0:T(8,128)(2,1)} copy(bf16[2,2048,1024]{2,1,0:T(8,128)(2,1)} %param.20) | data formatting | bytes 16777216 | tf_op args[9]
  320.4 5.6 %fusion = f32[2,2048]{1,0:T(2,128)S(1)} fusion(bf16[2,2048,1024]{1,2,0:T(8,128)(2,1)} %copy.14), kind=kLoop, calls=%fused_computation.2 | loop fusion | flops 12578816 | bytes 8404992 | tf_op jit(solution)/shard_map/reduce_sum | solution.py:36
  326.1 13.9 %psum.31 = f32[2048]{0:T(1024)S(1)} all-reduce(f32[2048]{0:T(1024)S(1)} %get-tuple-element.13), channel_id=1, replica_groups=mesh['ckpt'=8,'lat'=4] {'ckpt'}, use_global_device_ids=true, to_apply=%region_8.0 | all-reduce | flops 2048 | bytes 16384 | tf_op jit(solution)/shard_map/psum | solution.py:39
  340.1 55.4 %all-reduce.6.cloned.1.call-done = bf16[2,512,1024]{2,1,0:T(8,128)(2,1)} async-done(((bf16[2,512,1024]{2,1,0:T(8,128)(2,1)}), bf16[2,512,1024]{2,1,0:T(8,128)(2,1)}) %all-reduce.6.cloned.1.call-update) | async-done | bytes 2097168 | tf_op jit(solution)/shard_map/psum | solution.py:46
  395.4 10.5 %bitcast_convert_fusion = bf16[512,2048]{1,0:T(8,128)(2,1)} fusion(bf16[2,2048,1024]{2,1,0:T(8,128)(2,1)} %param.20, bf16[2,512,1024]{2,1,0:T(8,128)(2,1)} %all-gather.5.cloned.1.call-done, bf16[2,512,1024]{2,1,0:T(8,128)(2,1)} %all-reduce.6.cloned.1.call-done, f32[2,1024]{1,0:T(2,128)S(1)} %copy-done.10), kind=kOutput, calls=%fused_computation.24 | convolution fusion | flops 4302307328 | bytes 14688256 | tf_op jit(solution)/shard_map/ctd,cld->tl/dot_general | solution.py:53
  406.0 12.0 %fusion.3 = bf16[2,2048,1024]{1,2,0:T(8,128)(2,1)} fusion(bf16[2,2048,1024]{1,2,0:T(8,128)(2,1)} %copy.14, f32[2,2048]{1,0:T(2,128)S(1)} %get-tuple-element.12, f32[2048]{0:T(1024)S(1)} %broadcast_multiply_fusion, bf16[512,2048]{1,0:T(8,128)(2,1)S(1)} %get-tuple-element.9, bf16[2,512,1024]{2,1,0:T(8,128)(2,1)} %all-gather.5.cloned.1.call-done, ...), kind=kOutput, calls=%fused_computation.5 | convolution fusion | flops 4322230272 | bytes 23101440 | tf_op jit(solution)/shard_map/tl,ctd->cld/dot_general | solution.py:66
  418.0 11.9 %copy.17 = bf16[2,2048,1024]{2,1,0:T(8,128)(2,1)} copy(bf16[2,2048,1024]{1,2,0:T(8,128)(2,1)} %fusion.3) | data formatting | bytes 16777216
  429.9 36.5 %all-reduce.8.cloned.1.call-done = bf16[512,2048]{1,0:T(8,128)(2,1)} async-done(((bf16[512,2048]{1,0:T(8,128)(2,1)}), bf16[512,2048]{1,0:T(8,128)(2,1)}) %all-reduce.8.cloned.1.call-update) | async-done | bytes 2097168 | tf_op jit(solution)/shard_map/psum | solution.py:52
  466.5 4.4 convert_reduce_fusion.2
  470.8 6.8 %convolution_convert_fusion = bf16[2,1024,2048]{2,1,0:T(8,128)(2,1)} fusion(bf16[2,512,1024]{2,1,0:T(8,128)(2,1)S(1)} %copy-done.6, bf16[512,2048]{1,0:T(8,128)(2,1)S(1)} %get-tuple-element.11), kind=kOutput, calls=%fused_computation.7 | convolution fusion | flops 4299161600 | bytes 12582912 | tf_op jit(solution)/shard_map/ctd,tl->cdl/dot_general | solution.py:61
  (38 shorter events, 0.4 us)
Async XLA Ops:
  7.2 75.4 %copy-start = (f32[2,1024]{1,0:T(2,128)S(1)}, f32[2,1024]{1,0:T(2,128)}, u32[]{:S(2)}) copy-start(f32[2,1024]{1,0:T(2,128)} %param.17) | copy-start | bytes 24580
  7.2 55.8 %copy-start.9 = (f32[2,1024]{1,0:T(2,128)S(1)}, f32[2,1024]{1,0:T(2,128)}, u32[]{:S(2)}) copy-start(f32[2,1024]{1,0:T(2,128)} %param.15) | copy-start | bytes 24580
  7.2 55.8 %copy-start.7 = (f32[2,1024]{1,0:T(2,128)S(1)}, f32[2,1024]{1,0:T(2,128)}, u32[]{:S(2)}) copy-start(f32[2,1024]{1,0:T(2,128)} %param.13) | copy-start | bytes 24580
  7.2 55.8 %copy-start.8 = (f32[2,1024]{1,0:T(2,128)S(1)}, f32[2,1024]{1,0:T(2,128)}, u32[]{:S(2)}) copy-start(f32[2,1024]{1,0:T(2,128)} %param.12) | copy-start | bytes 24580
  7.2 51.4 %all-gather.3.cloned.1.call-start = ((), (), s32[]{:S(2)}) async-start(), calls=%async_computation.1 | async-start | bytes 2621440 | tf_op jit(solution)/shard_map/all_gather | solution.py:18
  7.9 149.6 %reduce-scatter.2.cloned.1.call-start = ((), (), s32[]{:S(2)}) async-start(), calls=%async_computation.2 | async-start | bytes 5242880 | tf_op jit(solution)/shard_map/reduce_scatter | solution.py:31
  58.6 4.4 copy-start.2
  63.0 6.1 %copy-start.5 = (bf16[2,1024,1024]{2,1,0:T(8,128)(2,1)S(1)}, bf16[2,1024,1024]{2,1,0:T(8,128)(2,1)}, u32[]{:S(2)}) copy-start(bf16[2,1024,1024]{2,1,0:T(8,128)(2,1)} %param.16) | copy-start | bytes 12582916
  82.4 75.2 %copy-start.3 = (bf16[2,512,256]{2,1,0:T(8,128)(2,1)S(1)}, bf16[2,512,256]{2,1,0:T(8,128)(2,1)}, u32[]{:S(2)}) copy-start(bf16[2,512,256]{2,1,0:T(8,128)(2,1)} %param.11) | copy-start | bytes 1572868
  82.5 124.3 %all-gather.5.cloned.1.call-start = ((), (), s32[]{:S(2)}) async-start(), calls=%async_computation.3 | async-start | bytes 2621440 | tf_op jit(solution)/shard_map/all_gather | solution.py:34
  159.8 136.9 %all-reduce.4.cloned.1.call-start = ((), (), s32[]{:S(2)}) async-start(), calls=%async_computation.4 | async-start | bytes 8388608 | tf_op jit(solution)/shard_map/psum | solution.py:39
  217.3 79.4 %copy-start.4 = (f32[2048]{0:T(1024)S(1)}, f32[2048]{0:T(1024)}, u32[]{:S(2)}) copy-start(f32[2048]{0:T(1024)} %param.19) | copy-start | bytes 24580
  217.3 178.2 %all-reduce.6.cloned.1.call-start = ((), (), s32[]{:S(2)}) async-start(), calls=%async_computation.5 | async-start | bytes 4194304 | tf_op jit(solution)/shard_map/psum | solution.py:46
  308.7 157.8 %all-reduce.8.cloned.1.call-start = ((), (), s32[]{:S(2)}) async-start(), calls=%async_computation.6 | async-start | bytes 4194304 | tf_op jit(solution)/shard_map/psum | solution.py:52
  320.4 75.1 %copy-start.10 = (f32[2,1024]{1,0:T(2,128)S(1)}, f32[2,1024]{1,0:T(2,128)}, u32[]{:S(2)}) copy-start(f32[2,1024]{1,0:T(2,128)} %param.21) | copy-start | bytes 24580
  429.9 40.9 %copy-start.6 = (bf16[2,512,1024]{2,1,0:T(8,128)(2,1)S(1)}, bf16[2,512,1024]{2,1,0:T(8,128)(2,1)}, u32[]{:S(2)}) copy-start(bf16[2,512,1024]{2,1,0:T(8,128)(2,1)} %all-gather.5.cloned.1.call-done) | copy-start | bytes 6291460
  470.8 6.8 %copy-start.1 = (f32[2,1024]{1,0:T(2,128)S(1)}, f32[2,1024]{1,0:T(2,128)}, u32[]{:S(2)}) copy-start(f32[2,1024]{1,0:T(2,128)} %param.17) | copy-start | bytes 24580
Sparse Core Ops, SparseCore 0:
  9.6 48.9 all-gather.2
  82.6 74.9 reduce-scatter.1
  159.9 46.7 all-gather.4
  217.4 79.2 all-reduce.3
  308.8 86.5 all-reduce.5
  406.1 60.3 all-reduce.7
where the time goes:
time: 485 us
  waiting for transfers between devices  344 us (71%)
  matrix products  68.4 us (14%)
  local copies, waits for them, and re-layouts  23.6 us (5%)
  other arithmetic  19.5 us (4%)
  between operations  14.3 us (3%)
  blocking collectives  13.9 us (3%)
    psum x1, waiting for transfers between devices, on_device(): lax.psum((jnp.einsum('ctd,cdl->tl', rows, w_enc, preferred_element_type=j...  79.2 us
    reduce_scatter x1, waiting for transfers between devices, on_device(): share = lax.psum_scatter(terms, 'lat', scatter_dimension=2, tiled=True)  75 us
    psum x1, waiting for transfers between devices, on_device(): lax.psum(recon_terms.astype(jnp.bfloat16), 'lat').astype(jnp.float32)  55.4 us
    all_gather x1, waiting for transfers between devices, on_device(): whole = lax.all_gather(hidden_in, 'lat', axis=2, tiled=True)  50.6 us
    all_gather x1, waiting for transfers between devices, on_device(): acts = lax.all_gather(piece, 'lat', axis=2, tiled=True)  46.9 us
    psum x1, waiting for transfers between devices, on_device(): lax.psum(jnp.einsum('ctd,cld->tl', rows, w_dec, preferred_element_type=jn...  36.5 us
    unnamed x24, local copies, waits for them, and re-layouts  23.6 us
    psum x1, blocking collectives, on_device(): lax.psum((jnp.einsum('ctd,cdl->tl', rows, w_enc, preferred_element_type=j...  13.9 us
  transfers between devices with their start and end apart: 6, of which 6 were waited for; matrix products, arithmetic and copies ran while one was open for 9% of the time, Pallas kernels for 0%

commit v1 on v0

v1 whole, which is shorter than its diff:
```python
import functools
import math

import jax
import jax.numpy as jnp
from jax import lax
from jax.experimental import pallas as pl
from jax.experimental.pallas import tpu as pltpu
from jax.sharding import PartitionSpec as P

norm_eps = 1e-05
row_eps = 1e-06
sparsity_weight = 0.2
MESH = pl.DeviceIdType.MESH
BF = jnp.bfloat16
F32 = jnp.float32


def kernel(
    nl, nc, chunks, order,
    hid, gain, bias, w_in, b_in, w_out, b_out, w_enc, b_enc, w_dec, b_dec, total,
    acts, dres, feat, dpre,
    full, vin, vout, venc, vdec, normed, active, part, part2, zbuf, ppart, dpart, cbuf, pre,
    wsem, own_sem, zsend, zrecv, csend, crecv,
):
    K, tok, cols = hid.shape
    D = cols * nl
    T = tok // chunks
    zr = T // nl
    cr = T // nc
    ff = vin.shape[2]
    lat = venc.shape[2]
    scale = 1.0 / math.sqrt(tok)
    lz = lax.axis_index("lat")
    lc = lax.axis_index("ckpt")

    barrier = pltpu.get_barrier_semaphore()
    for off in range(1, nl):
        pl.semaphore_signal(
            barrier, inc=1, device_id={"lat": lax.rem(lz + off, nl)}, device_id_type=MESH
        )
    for off in range(1, nc):
        pl.semaphore_signal(
            barrier, inc=1, device_id={"ckpt": lax.rem(lc + off, nc)}, device_id_type=MESH
        )
    pl.semaphore_wait(barrier, nl + nc - 2)

    def zcopy(stage, c, off, src, dst):
        return pltpu.make_async_remote_copy(
            src_ref=src, dst_ref=dst,
            send_sem=zsend.at[stage, c, off - 1], recv_sem=zrecv.at[stage, c, off - 1],
            device_id={"lat": lax.rem(lz + off, nl)}, device_id_type=MESH,
        )

    def ccopy(stage, c, off, src, dst):
        return pltpu.make_async_remote_copy(
            src_ref=src, dst_ref=dst,
            send_sem=csend.at[stage, c, off - 1], recv_sem=crecv.at[stage, c, off - 1],
            device_id={"ckpt": lax.rem(lc + off, nc)}, device_id_type=MESH,
        )

    def rows(c):
        return pl.ds(c * T, T)

    def zrows(c, i):
        return pl.ds(pl.multiple_of(c * T + i * zr, zr), zr)

    def crows(c, i):
        return pl.ds(pl.multiple_of(c * T + i * cr, cr), cr)

    def hid_copy(c, off):
        mine = pl.ds(pl.multiple_of(lz * cols, cols), cols)
        return zcopy(0, c, off, hid.at[:, rows(c), :], full.at[:, rows(c), mine])

    def zscatter(stage, slot, source):
        def make(c, off):
            dest = lax.rem(lz + off, nl)
            return zcopy(stage, c, off, source.at[:, zrows(c, dest), :], zbuf.at[slot, c, off - 1])
        return make

    def zgather(stage, ref):
        def make(c, off):
            piece = ref.at[:, zrows(c, lz), :]
            return zcopy(stage, c, off, piece, piece)
        return make

    def cscatter(stage, slot, source):
        def make(c, off):
            dest = lax.rem(lc + off, nc)
            return ccopy(stage, c, off, source.at[crows(c, dest), :], cbuf.at[slot, c, off - 1])
        return make

    def cgather(stage, ref):
        def make(c, off):
            piece = ref.at[crows(c, lc), :]
            return ccopy(stage, c, off, piece, piece)
        return make

    moves = {
        0: (hid_copy, nl),
        1: (zscatter(1, 0, part), nl),
        2: (zgather(2, acts), nl),
        3: (cscatter(0, 0, ppart), nc),
        4: (cgather(1, feat), nc),
        5: (zscatter(3, 1, part2), nl),
        6: (zgather(4, dres), nl),
        7: (cscatter(2, 1, dpart), nc),
        8: (cgather(3, dpre), nc),
    }

    def send(stage, c):
        make, n = moves[stage]
        for off in range(1, n):
            make(c, off).start()

    def recv(stage, c):
        make, n = moves[stage]
        for off in range(1, n):
            make(c, off).wait_recv()

    own = pltpu.make_async_copy(
        hid, full.at[:, :, pl.ds(pl.multiple_of(lz * cols, cols), cols)], own_sem
    )
    loads = [
        pltpu.make_async_copy(src, dst, wsem.at[i])
        for i, (src, dst) in enumerate(
            ((w_in, vin), (w_out, vout), (w_enc, venc), (w_dec, vdec))
        )
    ]
    for c in range(chunks):
        send(0, c)
    own.start()
    for load in loads:
        load.start()

    ft = min(256, ff)
    dt = min(256, D)
    lt = min(256, lat)

    def tile(i, t):
        return pl.ds(pl.multiple_of(i * t, t), t)

    def mlp(c):
        if c == 0:
            own.wait()
        recv(0, c)
        if c == 0:
            loads[0].wait()
            loads[1].wait()
        for k in range(K):
            floats = full[k, rows(c), :].astype(F32)
            center = floats - jnp.mean(floats, -1, keepdims=True)
            spread = jnp.mean(center * center, -1, keepdims=True)
            normed[...] = (
                center * lax.rsqrt(spread + norm_eps) * gain[k : k + 1, :] + bias[k : k + 1, :]
            ).astype(BF)

            @pl.loop(0, ff // ft)
            def _(i):
                s = tile(i, ft)
                h = jnp.dot(normed[...], vin[k, :, s], preferred_element_type=F32)
                h = h + b_in[k : k + 1, s]
                active[:, s] = (0.5 * h * (1.0 + lax.erf(h * math.sqrt(0.5)))).astype(BF)

            @pl.loop(0, D // dt)
            def _(i):
                s = tile(i, dt)
                part[k, rows(c), s] = jnp.dot(
                    active[...], vout[k, :, s], preferred_element_type=F32
                ).astype(BF)
        send(1, c)

    def make_acts(c):
        recv(1, c)
        for k in range(K):
            mine = zrows(c, lz)
            value = part[k, mine, :].astype(F32)
            for off in range(1, nl):
                value = value + zbuf[0, c, off - 1, k].astype(F32)
            value = value + full[k, mine, :].astype(F32) + b_out[k : k + 1, :]
            acts[k, mine, :] = value.astype(BF)
        send(2, c)

    def encode(c):
        recv(2, c)
        if c == 0:
            loads[2].wait()

        @pl.loop(0, lat // lt)
        def _(i):
            s = tile(i, lt)
            value = jnp.dot(acts[0, rows(c), :], venc[0, :, s], preferred_element_type=F32)
            for k in range(1, K):
                value = value + jnp.dot(
                    acts[k, rows(c), :], venc[k, :, s], preferred_element_type=F32
                )
            ppart[rows(c), s] = value.astype(ppart.dtype)
        send(3, c)

    def make_feat(c):
        recv(3, c)
        value = ppart[crows(c, lc), :].astype(F32)
        for off in range(1, nc):
            value = value + cbuf[0, c, off - 1].astype(F32)
        value = value + b_enc[...]
        pre[c] = value
        feat[crows(c, lc), :] = jnp.maximum(value, 0.0).astype(BF)
        send(4, c)

    def decode(c):
        recv(4, c)
        if c == 0:
            loads[3].wait()
        for k in range(K):

            @pl.loop(0, D // dt)
            def _(i):
                s = tile(i, dt)
                part2[k, rows(c), s] = jnp.dot(
                    feat[rows(c), :], vdec[k, :, s], preferred_element_type=F32
                ).astype(BF)
        send(5, c)

    def make_dres(c):
        recv(5, c)
        for k in range(K):
            mine = zrows(c, lz)
            value = part2[k, mine, :].astype(F32)
            for off in range(1, nl):
                value = value + zbuf[1, c, off - 1, k].astype(F32)
            value = value + b_dec[k : k + 1, :] - acts[k, mine, :].astype(F32)
            dres[k, mine, :] = (value * scale).astype(BF)
        send(6, c)

    def back(c):
        recv(6, c)
        dims = (((1,), (1,)), ((), ()))

        @pl.loop(0, lat // lt)
        def _(i):
            s = tile(i, lt)
            value = sparsity_weight * scale * total[:, s]
            for k in range(K):
                value = value + lax.dot_general(
                    dres[k, rows(c), :], vdec[k, s, :], dims, preferred_element_type=F32
                )
            dpart[rows(c), s] = value.astype(BF)
        send(7, c)

    def make_dpre(c):
        recv(7, c)
        value = dpart[crows(c, lc), :].astype(F32)
        for off in range(1, nc):
            value = value + cbuf[1, c, off - 1].astype(F32)
        dpre[crows(c, lc), :] = jnp.where(pre[c] > 0.0, value, 0.0).astype(BF)
        send(8, c)

    def last(c):
        recv(8, c)

    steps = (mlp, make_acts, encode, make_feat, decode, make_dres, back, make_dpre, last)
    for step, c in order:
        steps[step](c)
    for stage, (make, n) in moves.items():
        for c in range(chunks):
            for off in range(1, n):
                make(c, off).wait_send()


def fused(hidden_in, ln_gain, ln_bias, w_in, b_in, w_out, b_out, w_enc, b_enc, w_dec, b_dec, total,
          nl, nc, chunks, skew):
    K, tok, cols = hidden_in.shape
    D = cols * nl
    ff = w_in.shape[2]
    lat = w_enc.shape[2]
    T = tok // chunks
    steps = 9
    order = sorted(
        ((s, c) for s in range(steps) for c in range(chunks)), key=lambda p: (p[0] + skew * p[1], p[1])
    )
    VM = pl.BlockSpec(memory_space=pltpu.VMEM)
    HB = pl.BlockSpec(memory_space=pl.ANY)
    flops = 2 * tok * K * (2 * D * ff + 3 * D * lat)
    return pl.pallas_call(
        functools.partial(kernel, nl, nc, chunks, order),
        out_shape=(
            jax.ShapeDtypeStruct((K, tok, D), BF),
            jax.ShapeDtypeStruct((K, tok, D), BF),
            jax.ShapeDtypeStruct((tok, lat), BF),
            jax.ShapeDtypeStruct((tok, lat), BF),
        ),
        in_specs=[HB, VM, VM, HB, VM, HB, VM, HB, VM, HB, VM, VM],
        out_specs=(VM, VM, VM, VM),
        scratch_shapes=[
            pltpu.VMEM((K, tok, D), BF),
            pltpu.VMEM(w_in.shape, BF),
            pltpu.VMEM(w_out.shape, BF),
            pltpu.VMEM(w_enc.shape, BF),
            pltpu.VMEM(w_dec.shape, BF),
            pltpu.VMEM((T, D), BF),
            pltpu.VMEM((T, ff), BF),
            pltpu.VMEM((K, tok, D), BF),
            pltpu.VMEM((K, tok, D), BF),
            pltpu.VMEM((2, chunks, nl - 1, K, T // nl, D), BF),
            pltpu.VMEM((tok, lat), BF),
            pltpu.VMEM((tok, lat), BF),
            pltpu.VMEM((2, chunks, nc - 1, T // nc, lat), BF),
            pltpu.VMEM((chunks, T // nc, lat), F32),
            pltpu.SemaphoreType.DMA((4,)),
            pltpu.SemaphoreType.DMA,
            pltpu.SemaphoreType.DMA((5, chunks, nl - 1)),
            pltpu.SemaphoreType.DMA((5, chunks, nl - 1)),
            pltpu.SemaphoreType.DMA((4, chunks, nc - 1)),
            pltpu.SemaphoreType.DMA((4, chunks, nc - 1)),
        ],
        compiler_params=pltpu.CompilerParams(
            collective_id=0, has_side_effects=True, vmem_limit_bytes=62 * 1024 * 1024
        ),
        cost_estimate=pl.CostEstimate(flops=flops, bytes_accessed=40 << 20, transcendentals=tok * ff),
    )(hidden_in, ln_gain, ln_bias, w_in, b_in, w_out, b_out, w_enc, b_enc[None, :], w_dec, b_dec,
      total[None, :])


def plain(hidden_in, ln_gain, ln_bias, w_in, b_in, w_out, b_out, w_enc, b_enc, w_dec, b_dec, total):
    tokens = hidden_in.shape[1]
    feat_cols = hidden_in.shape[2]
    scale = 1.0 / math.sqrt(tokens)
    lat_index = lax.axis_index("lat")
    whole = lax.all_gather(hidden_in, "lat", axis=2, tiled=True)
    floats = whole.astype(F32)
    center = floats - jnp.mean(floats, -1, keepdims=True)
    spread = jnp.mean(center * center, -1, keepdims=True)
    normed = (
        center * lax.rsqrt(spread + norm_eps) * ln_gain[:, None, :] + ln_bias[:, None, :]
    ).astype(BF)
    raised = jnp.einsum("ctd,cdf->ctf", normed, w_in, preferred_element_type=F32) + b_in[:, None, :]
    active = jax.nn.gelu(raised, approximate=False).astype(BF)
    terms = jnp.einsum("ctf,cfd->ctd", active, w_out, preferred_element_type=F32)
    share = lax.psum_scatter(terms, "lat", scatter_dimension=2, tiled=True)
    out_bias = lax.dynamic_slice_in_dim(b_out, lat_index * feat_cols, feat_cols, 1)
    piece = (hidden_in.astype(F32) + share + out_bias[:, None, :]).astype(BF)
    acts = lax.all_gather(piece, "lat", axis=2, tiled=True)
    pre_sum, total = lax.psum(
        (jnp.einsum("ctd,cdl->tl", acts, w_enc, preferred_element_type=F32), total), "ckpt"
    )
    pre = pre_sum + b_enc[None, :]
    feat = jnp.maximum(pre, 0.0).astype(BF)
    recon_terms = jnp.einsum("tl,cld->ctd", feat, w_dec, preferred_element_type=F32)
    recon = lax.psum(recon_terms.astype(BF), "lat").astype(F32)
    dres = ((recon + b_dec[:, None, :] - acts.astype(F32)) * scale).astype(BF)
    dfeat = lax.psum(
        jnp.einsum("ctd,cld->tl", dres, w_dec, preferred_element_type=F32).astype(BF), "ckpt"
    ).astype(F32) + (sparsity_weight * scale * total)[None, :]
    dpre = jnp.where(pre > 0.0, dfeat, 0.0).astype(BF)
    return acts, dres, feat, dpre


def on_device(nl, nc, hidden_in, ln_gain, ln_bias, w_in, b_in, w_out, b_out, w_enc, b_enc, w_dec, b_dec):
    K, tok, cols = hidden_in.shape
    scale = 1.0 / math.sqrt(tok)
    chunks = 2
    T = tok // chunks
    wide_dec = w_dec.astype(F32)
    norms = jnp.sqrt(jnp.sum(wide_dec * wide_dec, 2) + row_eps)
    local_total = jnp.sum(norms, 0)
    args = (hidden_in, ln_gain, ln_bias, w_in, b_in, w_out, b_out, w_enc, b_enc, w_dec, b_dec,
            local_total)
    if cols % 128 == 0 and T % (16 * nl) == 0 and T % (16 * nc) == 0:
        acts, dres, feat, dpre = fused(*args, nl, nc, chunks, 2)
    else:
        acts, dres, feat, dpre = plain(*args)
    grad_enc = jnp.einsum("ctd,tl->cdl", acts, dpre, preferred_element_type=F32).astype(BF)
    grad_benc = jnp.sum(dpre.astype(F32), 0)
    column = jnp.sum(feat.astype(F32), 0)
    main = jnp.einsum("tl,ctd->cld", feat, dres, preferred_element_type=F32)
    extra = sparsity_weight * scale * column[None, :, None] * wide_dec / norms[:, :, None]
    grad_dec = (main + extra).astype(BF)
    return (grad_enc, grad_benc, grad_dec)


def solution(mesh):
    placed = (
        P("ckpt", None, "lat"),
        P("ckpt", None),
        P("ckpt", None),
        P("ckpt", None, "lat"),
        P("ckpt", "lat"),
        P("ckpt", "lat", None),
        P("ckpt", None),
        P("ckpt", None, "lat"),
        P("lat"),
        P("ckpt", "lat", None),
        P("ckpt", None),
    )
    return jax.shard_map(
        functools.partial(on_device, mesh.shape["lat"], mesh.shape["ckpt"]),
        mesh=mesh,
        in_specs=placed,
        out_specs=(P("ckpt", None, "lat"), P("lat"), P("ckpt", "lat", None)),
        check_vma=False,
    )
```

time: 485 us -> 341 us (0.70)
  waiting for transfers between devices: 344 us -> 0 us
  Pallas kernels: 0 us -> 284 us
  matrix products: 68.4 us -> 18.6 us
  blocking collectives: 13.9 us -> 0 us
  between operations: 14.3 us -> 0.66 us
  other arithmetic: 19.5 us -> 9.97 us
    pallas_call x0 -> x1, Pallas kernels: none -> 284 us  [fused(): pl.pallas_call(functools.partial(kernel, nl, nc, chunks, order), out_shap...]
    psum x3 -> x0, waiting for transfers between devices: 171 us -> none  [the longest x1 79.2 us: on_device(): lax.psum((jnp.einsum('ctd,cdl->tl', rows, w_enc, preferred_element_type=j...]
    all_gather x2 -> x0, waiting for transfers between devices: 97.4 us -> none  [the longest x1 50.6 us: on_device(): whole = lax.all_gather(hidden_in, 'lat', axis=2, tiled=True)]
    reduce_scatter x1 -> x0, waiting for transfers between devices: 75 us -> none  [on_device(): share = lax.psum_scatter(terms, 'lat', scatter_dimension=2, tiled=True)]
    dot_general x7 -> x2, matrix products: 68.4 us -> 18.6 us  [the longest x1 10.2 us: on_device(): main = jnp.einsum('tl,ctd->cld', feat, dres, preferred_element_type=F32)]
    psum x1 -> x0, blocking collectives: 13.9 us -> none  [on_device(): lax.psum((jnp.einsum('ctd,cdl->tl', rows, w_enc, preferred_element_type=j...]
    reduce_sum x4 -> x1, other arithmetic: 11.6 us -> 3.75 us  [on_device(): column = jnp.sum(feat.astype(F32), 0)]
    unnamed x24 -> x8, local copies, waits for them, and re-layouts: 23.6 us -> 23.6 us
  transfers between devices with their start and end apart: 6 -> 0, of which waited for: 6 -> 0; matrix products, arithmetic and copies ran while one was open for 9% -> 0% of each run, Pallas kernels for 0% -> 0%
where the time goes in v1:
time: 341 us; the launch traced here: 337 us
  Pallas kernels  284 us (83%)
  local copies, waits for them, and re-layouts  23.6 us (7%)
  matrix products  18.6 us (5%)
  other arithmetic  9.97 us (3%)
    pallas_call x1, Pallas kernels, fused(): pl.pallas_call(functools.partial(kernel, nl, nc, chunks, order), out_shap...  284 us
    unnamed x8, local copies, waits for them, and re-layouts  23.6 us
    dot_general x1, matrix products, on_device(): main = jnp.einsum('tl,ctd->cld', feat, dres, preferred_element_type=F32)  10.2 us
    dot_general x1, matrix products, on_device(): jnp.einsum('ctd,tl->cdl', acts, dpre, preferred_element_type=F32).astype(BF)  8.38 us

profile of v1, /device:TPU:0, one launch (start us, length us, event | category | flops | bytes accessed | tf_op | source)
XLA Modules:
  0.0 336.8 jit_solution(5132788921766484774)
XLA Ops:
  0.6 11.6 %copy.14 = bf16[2,2048,1024]{1,2,0:T(8,128)(2,1)} copy(bf16[2,2048,1024]{2,1,0:T(8,128)(2,1)} %w_dec.1) | data formatting | bytes 16777216 | tf_op args[9]
  12.2 5.6 %fusion = f32[2,2048]{1,0:T(2,128)S(1)} fusion(bf16[2,2048,1024]{1,2,0:T(8,128)(2,1)} %copy.14), kind=kLoop, calls=%fused_computation.2 | loop fusion | flops 12578816 | bytes 8404992 | tf_op jit(solution)/shard_map/reduce_sum | solution.py:364
  17.8 0.6 add_sqrt_fusion
  18.4 284.1 %shard_map.130 = (bf16[2,512,1024]{2,1,0:T(8,128)(2,1)}, bf16[2,512,1024]{2,1,0:T(8,128)(2,1)}, bf16[512,2048]{1,0:T(8,128)(2,1)}, bf16[512,2048]{1,0:T(8,128)(2,1)}) custom-call(bf16[2,512,256]{2,1,0:T(8,128)(2,1)} %hid.1, f32[2,1024]{1,0:T(2,128)} %gain.1, f32[2,1024]{1,0:T(2,128)} %bias.1, bf16[2,1024,1024]{2,1,0:T(8,128)(2,1)} %w_in.1, f32[2,1024]{1,0:T(2,128)} %b_in.1, ...), custom_call_target="tpu_custom_call" | custom-call | flops 17179869184 | bytes 41943040 | tf_op jit(solution)/shard_map/pallas_call | solution.py:284
  302.5 0.0 copy-start.1
  302.5 0.0 copy-start.2
  302.5 3.8 %convert_reduce_fusion = (f32[2048]{0:T(1024)S(1)}, f32[2048]{0:T(1024)}) fusion(bf16[512,2048]{1,0:T(8,128)(2,1)} %get-tuple-element.10, bf16[512,2048]{1,0:T(8,128)(2,1)} %get-tuple-element.8), kind=kLoop, calls=%fused_computation.7 | loop fusion | flops 4190208 | bytes 4210688 | tf_op jit(solution)/shard_map/reduce_sum | solution.py:374
  306.3 0.0 copy-done.1
  306.3 0.0 copy-done.2
  306.3 10.2 %fusion.3 = bf16[2,2048,1024]{1,2,0:T(8,128)(2,1)} fusion(bf16[2,2048,1024]{1,2,0:T(8,128)(2,1)} %copy.14, f32[2,2048]{1,0:T(2,128)S(1)} %get-tuple-element.14, f32[2048]{0:T(1024)S(1)} %broadcast_multiply_fusion, bf16[2,512,1024]{2,1,0:T(8,128)(2,1)S(1)} %copy-done.2, bf16[512,2048]{1,0:T(8,128)(2,1)S(1)} %copy-done.1), kind=kOutput, calls=%fused_computation.5 | convolution fusion | flops 4315938816 | bytes 20996096 | tf_op jit(solution)/shard_map/tl,ctd->cld/dot_general | solution.py:375
  316.5 0.0 copy-start
  316.5 12.0 %copy.17 = bf16[2,2048,1024]{2,1,0:T(8,128)(2,1)} copy(bf16[2,2048,1024]{1,2,0:T(8,128)(2,1)} %fusion.3) | data formatting | bytes 16777216
  328.5 0.0 copy-done
  328.5 8.4 %convolution_convert_fusion = bf16[2,1024,2048]{2,1,0:T(8,128)(2,1)} fusion(bf16[2,512,1024]{2,1,0:T(8,128)(2,1)} %get-tuple-element.7, bf16[512,2048]{1,0:T(8,128)(2,1)S(1)} %copy-done), kind=kOutput, calls=%fused_computation.6 | convolution fusion | flops 4299161600 | bytes 12582912 | tf_op jit(solution)/shard_map/ctd,tl->cdl/dot_general | solution.py:372
  (1 shorter events, 0.0 us)
Async XLA Ops:
  302.5 3.8 %copy-start.1 = (bf16[512,2048]{1,0:T(8,128)(2,1)S(1)}, bf16[512,2048]{1,0:T(8,128)(2,1)}, u32[]{:S(2)}) copy-start(bf16[512,2048]{1,0:T(8,128)(2,1)} %get-tuple-element.10) | copy-start | bytes 6291460
  302.5 3.8 %copy-start.2 = (bf16[2,512,1024]{2,1,0:T(8,128)(2,1)S(1)}, bf16[2,512,1024]{2,1,0:T(8,128)(2,1)}, u32[]{:S(2)}) copy-start(bf16[2,512,1024]{2,1,0:T(8,128)(2,1)} %get-tuple-element.9) | copy-start | bytes 6291460
  316.5 12.0 %copy-start = (bf16[512,2048]{1,0:T(8,128)(2,1)S(1)}, bf16[512,2048]{1,0:T(8,128)(2,1)}, u32[]{:S(2)}) copy-start(bf16[512,2048]{1,0:T(8,128)(2,1)} %get-tuple-element.8) | copy-start | bytes 6291460

commit v2 on v1

--- a/solution.py
+++ b/solution.py
@@ -18,9 +18,9 @@
 
 def kernel(
     nl, nc, chunks, order,
-    hid, gain, bias, w_in, b_in, w_out, b_out, w_enc, b_enc, w_dec, b_dec, total,
+    hid, gain, bias, w_in, b_in, w_out, b_out, w_enc, b_enc, w_dec, b_dec,
     acts, dres, feat, dpre,
-    full, vin, vout, venc, vdec, normed, active, part, part2, zbuf, ppart, dpart, cbuf, pre,
+    full, vin, vout, venc, vdec, normed, active, part, part2, zbuf, ppart, dpart, cbuf, pre, total,
     wsem, own_sem, zsend, zrecv, csend, crecv,
 ):
     K, tok, cols = hid.shape
@@ -45,10 +45,10 @@
         )
     pl.semaphore_wait(barrier, nl + nc - 2)
 
-    def zcopy(stage, c, off, src, dst):
+    def zcopy(stage, c, k, off, src, dst):
         return pltpu.make_async_remote_copy(
             src_ref=src, dst_ref=dst,
-            send_sem=zsend.at[stage, c, off - 1], recv_sem=zrecv.at[stage, c, off - 1],
+            send_sem=zsend.at[stage, c, k, off - 1], recv_sem=zrecv.at[stage, c, k, off - 1],
             device_id={"lat": lax.rem(lz + off, nl)}, device_id_type=MESH,
         )
 
@@ -68,30 +68,32 @@
     def crows(c, i):
         return pl.ds(pl.multiple_of(c * T + i * cr, cr), cr)
 
-    def hid_copy(c, off):
+    def hid_copy(c, k, off):
         mine = pl.ds(pl.multiple_of(lz * cols, cols), cols)
-        return zcopy(0, c, off, hid.at[:, rows(c), :], full.at[:, rows(c), mine])
+        return zcopy(0, c, k, off, hid.at[k, rows(c), :], full.at[k, rows(c), mine])
 
     def zscatter(stage, slot, source):
-        def make(c, off):
+        def make(c, k, off):
             dest = lax.rem(lz + off, nl)
-            return zcopy(stage, c, off, source.at[:, zrows(c, dest), :], zbuf.at[slot, c, off - 1])
+            return zcopy(
+                stage, c, k, off, source.at[k, zrows(c, dest), :], zbuf.at[slot, c, off - 1, k]
+            )
         return make
 
     def zgather(stage, ref):
-        def make(c, off):
-            piece = ref.at[:, zrows(c, lz), :]
-            return zcopy(stage, c, off, piece, piece)
+        def make(c, k, off):
+            piece = ref.at[k, zrows(c, lz), :]
+            return zcopy(stage, c, k, off, piece, piece)
         return make
 
     def cscatter(stage, slot, source):
-        def make(c, off):
+        def make(c, k, off):
             dest = lax.rem(lc + off, nc)
             return ccopy(stage, c, off, source.at[crows(c, dest), :], cbuf.at[slot, c, off - 1])
         return make
 
     def cgather(stage, ref):
-        def make(c, off):
+        def make(c, k, off):
             piece = ref.at[crows(c, lc), :]
             return ccopy(stage, c, off, piece, piece)
         return make
@@ -108,15 +110,17 @@
         8: (cgather(3, dpre), nc),
     }
 
-    def send(stage, c):
+    parts = {stage: K if stage in (0, 1, 2, 5, 6) else 1 for stage in moves}
+
+    def send(stage, c, k=0):
         make, n = moves[stage]
         for off in range(1, n):
-            make(c, off).start()
-
-    def recv(stage, c):
+            make(c, k, off).start()
+
+    def recv(stage, c, k=0):
         make, n = moves[stage]
         for off in range(1, n):
-            make(c, off).wait_recv()
+            make(c, k, off).wait_recv()
 
     own = pltpu.make_async_copy(
         hid, full.at[:, :, pl.ds(pl.multiple_of(lz * cols, cols), cols)], own_sem
@@ -128,7 +132,8 @@
         )
     ]
     for c in range(chunks):
-        send(0, c)
+        for k in range(K):
+            send(0, c, k)
     own.start()
     for load in loads:
         load.start()
@@ -140,14 +145,24 @@
     def tile(i, t):
         return pl.ds(pl.multiple_of(i * t, t), t)
 
+    def add_norms():
+        @pl.loop(0, lat // lt)
+        def _(i):
+            s = tile(i, lt)
+            value = jnp.zeros((lt, 1), F32)
+            for k in range(K):
+                w = vdec[k, s, :].astype(F32)
+                value = value + jnp.sqrt(jnp.sum(w * w, -1, keepdims=True) + row_eps)
+            total[:, s] = jnp.broadcast_to(value, (lt, 128)).T[0:8, :]
+
     def mlp(c):
         if c == 0:
             own.wait()
-        recv(0, c)
-        if c == 0:
-            loads[0].wait()
-            loads[1].wait()
-        for k in range(K):
+            for load in loads:
+                load.wait()
+            add_norms()
+        for k in range(K):
+            recv(0, c, k)
             floats = full[k, rows(c), :].astype(F32)
             center = floats - jnp.mean(floats, -1, keepdims=True)
             spread = jnp.mean(center * center, -1, keepdims=True)
@@ -168,23 +183,23 @@
                 part[k, rows(c), s] = jnp.dot(
                     active[...], vout[k, :, s], preferred_element_type=F32
                 ).astype(BF)
-        send(1, c)
+
+            send(1, c, k)
 
     def make_acts(c):
-        recv(1, c)
-        for k in range(K):
+        for k in range(K):
+            recv(1, c, k)
             mine = zrows(c, lz)
             value = part[k, mine, :].astype(F32)
             for off in range(1, nl):
                 value = value + zbuf[0, c, off - 1, k].astype(F32)
             value = value + full[k, mine, :].astype(F32) + b_out[k : k + 1, :]
             acts[k, mine, :] = value.astype(BF)
-        send(2, c)
+            send(2, c, k)
 
     def encode(c):
-        recv(2, c)
-        if c == 0:
-            loads[2].wait()
+        for k in range(K):
+            recv(2, c, k)
 
         @pl.loop(0, lat // lt)
         def _(i):
@@ -209,8 +224,6 @@
 
     def decode(c):
         recv(4, c)
-        if c == 0:
-            loads[3].wait()
         for k in range(K):
 
             @pl.loop(0, D // dt)
@@ -219,27 +232,29 @@
                 part2[k, rows(c), s] = jnp.dot(
                     feat[rows(c), :], vdec[k, :, s], preferred_element_type=F32
                 ).astype(BF)
-        send(5, c)
+
+            send(5, c, k)
 
     def make_dres(c):
-        recv(5, c)
-        for k in range(K):
+        for k in range(K):
+            recv(5, c, k)
             mine = zrows(c, lz)
             value = part2[k, mine, :].astype(F32)
             for off in range(1, nl):
                 value = value + zbuf[1, c, off - 1, k].astype(F32)
             value = value + b_dec[k : k + 1, :] - acts[k, mine, :].astype(F32)
             dres[k, mine, :] = (value * scale).astype(BF)
-        send(6, c)
+            send(6, c, k)
 
     def back(c):
-        recv(6, c)
+        for k in range(K):
+            recv(6, c, k)
         dims = (((1,), (1,)), ((), ()))
 
         @pl.loop(0, lat // lt)
         def _(i):
             s = tile(i, lt)
-            value = sparsity_weight * scale * total[:, s]
+            value = sparsity_weight * scale * total[0:1, s]
             for k in range(K):
                 value = value + lax.dot_general(
                     dres[k, rows(c), :], vdec[k, s, :], dims, preferred_element_type=F32
@@ -263,11 +278,12 @@
         steps[step](c)
     for stage, (make, n) in moves.items():
         for c in range(chunks):
-            for off in range(1, n):
-                make(c, off).wait_send()
-
-
-def fused(hidden_in, ln_gain, ln_bias, w_in, b_in, w_out, b_out, w_enc, b_enc, w_dec, b_dec, total,
+            for k in range(parts[stage]):
+                for off in range(1, n):
+                    make(c, k, off).wait_send()
+
+
+def fused(hidden_in, ln_gain, ln_bias, w_in, b_in, w_out, b_out, w_enc, b_enc, w_dec, b_dec,
           nl, nc, chunks, skew):
     K, tok, cols = hidden_in.shape
     D = cols * nl
@@ -289,7 +305,7 @@
             jax.ShapeDtypeStruct((tok, lat), BF),
             jax.ShapeDtypeStruct((tok, lat), BF),
         ),
-        in_specs=[HB, VM, VM, HB, VM, HB, VM, HB, VM, HB, VM, VM],
+        in_specs=[HB, VM, VM, HB, VM, HB, VM, HB, VM, HB, VM],
         out_specs=(VM, VM, VM, VM),
         scratch_shapes=[
             pltpu.VMEM((K, tok, D), BF),
@@ -306,10 +322,11 @@
             pltpu.VMEM((tok, lat), BF),
             pltpu.VMEM((2, chunks, nc - 1, T // nc, lat), BF),
             pltpu.VMEM((chunks, T // nc, lat), F32),
+            pltpu.VMEM((8, lat), F32),
             pltpu.SemaphoreType.DMA((4,)),
             pltpu.SemaphoreType.DMA,
-            pltpu.SemaphoreType.DMA((5, chunks, nl - 1)),
-            pltpu.SemaphoreType.DMA((5, chunks, nl - 1)),
+            pltpu.SemaphoreType.DMA((5, chunks, K, nl - 1)),
+            pltpu.SemaphoreType.DMA((5, chunks, K, nl - 1)),
             pltpu.SemaphoreType.DMA((4, chunks, nc - 1)),
             pltpu.SemaphoreType.DMA((4, chunks, nc - 1)),
         ],
@@ -317,8 +334,56 @@
             collective_id=0, has_side_effects=True, vmem_limit_bytes=62 * 1024 * 1024
         ),
         cost_estimate=pl.CostEstimate(flops=flops, bytes_accessed=40 << 20, transcendentals=tok * ff),
-    )(hidden_in, ln_gain, ln_bias, w_in, b_in, w_out, b_out, w_enc, b_enc[None, :], w_dec, b_dec,
-      total[None, :])
+    )(hidden_in, ln_gain, ln_bias, w_in, b_in, w_out, b_out, w_enc, b_enc[None, :], w_dec, b_dec)
+
+
+def grads_kernel(acts, dres, feat, dpre, w_dec, genc, gbenc, gdec, flipped):
+    K, tok, D = acts.shape
+    scale = 1.0 / math.sqrt(tok)
+
+    @pl.when(pl.program_id(0) == 0)
+    def _():
+        for k in range(K):
+            flipped[k] = acts[k].T
+
+    d = dpre[...]
+    gbenc[...] = jnp.sum(d.astype(F32), 0, keepdims=True)
+    for k in range(K):
+        genc[k] = jnp.dot(flipped[k], d, preferred_element_type=F32).astype(BF)
+    f = feat[...].T
+    column = jnp.dot(f, jnp.ones((tok, 128), BF), preferred_element_type=F32)[:, 0:1]
+    for k in range(K):
+        w = w_dec[k].astype(F32)
+        norms = jnp.sqrt(jnp.sum(w * w, -1, keepdims=True) + row_eps)
+        main = jnp.dot(f, dres[k], preferred_element_type=F32)
+        gdec[k] = (main + (sparsity_weight * scale * column / norms) * w).astype(BF)
+
+
+def grads(acts, dres, feat, dpre, w_dec):
+    K, tok, D = acts.shape
+    lat = feat.shape[1]
+    lt = min(256, lat)
+    whole = pl.BlockSpec((K, tok, D), lambda i: (0, 0, 0))
+    cols = pl.BlockSpec((tok, lt), lambda i: (0, i))
+    deep = pl.BlockSpec((K, lt, D), lambda i: (0, i, 0))
+    genc, gbenc, gdec = pl.pallas_call(
+        grads_kernel,
+        grid=(lat // lt,),
+        out_shape=(
+            jax.ShapeDtypeStruct((K, D, lat), BF),
+            jax.ShapeDtypeStruct((1, lat), F32),
+            jax.ShapeDtypeStruct((K, lat, D), BF),
+        ),
+        in_specs=[whole, whole, cols, cols, deep],
+        out_specs=(
+            pl.BlockSpec((K, D, lt), lambda i: (0, 0, i)),
+            pl.BlockSpec((1, lt), lambda i: (0, i)),
+            deep,
+        ),
+        scratch_shapes=[pltpu.VMEM((K, D, tok), BF)],
+        compiler_params=pltpu.CompilerParams(vmem_limit_bytes=48 * 1024 * 1024),
+    )(acts, dres, feat, dpre, w_dec)
+    return genc, gbenc[0], gdec
 
 
 def plain(hidden_in, ln_gain, ln_bias, w_in, b_in, w_out, b_out, w_enc, b_enc, w_dec, b_dec, total):
@@ -360,15 +425,12 @@
     scale = 1.0 / math.sqrt(tok)
     chunks = 2
     T = tok // chunks
+    args = (hidden_in, ln_gain, ln_bias, w_in, b_in, w_out, b_out, w_enc, b_enc, w_dec, b_dec)
+    if cols % 128 == 0 and T % (16 * nl) == 0 and T % (16 * nc) == 0:
+        return grads(*fused(*args, nl, nc, chunks, 2), w_dec)
     wide_dec = w_dec.astype(F32)
     norms = jnp.sqrt(jnp.sum(wide_dec * wide_dec, 2) + row_eps)
-    local_total = jnp.sum(norms, 0)
-    args = (hidden_in, ln_gain, ln_bias, w_in, b_in, w_out, b_out, w_enc, b_enc, w_dec, b_dec,
-            local_total)
-    if cols % 128 == 0 and T % (16 * nl) == 0 and T % (16 * nc) == 0:
-        acts, dres, feat, dpre = fused(*args, nl, nc, chunks, 2)
-    else:
-        acts, dres, feat, dpre = plain(*args)
+    acts, dres, feat, dpre = plain(*args, jnp.sum(norms, 0))
     grad_enc = jnp.einsum("ctd,tl->cdl", acts, dpre, preferred_element_type=F32).astype(BF)
     grad_benc = jnp.sum(dpre.astype(F32), 0)
     column = jnp.sum(feat.astype(F32), 0)

time: 341 us -> 302 us (0.89)
  local copies, waits for them, and re-layouts: 23.6 us -> 3.17 us
  matrix products: 18.6 us -> 0 us
  Pallas kernels: 284 us -> 294 us
  other arithmetic: 9.97 us -> 0 us
    unnamed x8 -> x4, local copies, waits for them, and re-layouts: 23.6 us -> 3.17 us
    dot_general x2 -> x0, matrix products: 18.6 us -> none  [the longest x1 10.2 us: on_device(): main = jnp.einsum('tl,ctd->cld', feat, dres, preferred_element_type=F32)]
    pallas_call x0 -> x1, Pallas kernels: none -> 16.1 us  [grads(): pl.pallas_call(grads_kernel, grid=(lat // lt,), out_shape=(jax.ShapeDtype...]
    reduce_sum x2 -> x0, other arithmetic: 9.32 us -> none  [the longest x1 5.57 us: on_device(): norms = jnp.sqrt(jnp.sum(wide_dec * wide_dec, 2) + row_eps)]
    pallas_call x1, Pallas kernels: 284 us -> 278 us  [fused(): pl.pallas_call(functools.partial(kernel, nl, nc, chunks, order), out_shap...]
where the time goes in v2:
time: 302 us; the launch traced here: 298 us
  Pallas kernels  294 us (97%)
  local copies, waits for them, and re-layouts  3.17 us (1%)
    pallas_call x1, Pallas kernels, fused(): pl.pallas_call(functools.partial(kernel, nl, nc, chunks, order), out_shap...  278 us
    pallas_call x1, Pallas kernels, grads(): pl.pallas_call(grads_kernel, grid=(lat // lt,), out_shape=(jax.ShapeDtype...  16.1 us

profile of v2, /device:TPU:0, one launch (start us, length us, event | category | flops | bytes accessed | tf_op | source)
XLA Modules:
  0.0 298.0 jit_solution(13858225889633539549)
XLA Ops:
  0.6 278.0 %shard_map.130 = (bf16[2,512,1024]{2,1,0:T(8,128)(2,1)}, bf16[2,512,1024]{2,1,0:T(8,128)(2,1)}, bf16[512,2048]{1,0:T(8,128)(2,1)}, bf16[512,2048]{1,0:T(8,128)(2,1)}) custom-call(bf16[2,512,256]{2,1,0:T(8,128)(2,1)} %hid.1, f32[2,1024]{1,0:T(2,128)} %gain.1, f32[2,1024]{1,0:T(2,128)} %bias.1, bf16[2,1024,1024]{2,1,0:T(8,128)(2,1)} %w_in.1, f32[2,1024]{1,0:T(2,128)} %b_in.1, ...), custom_call_target="tpu_custom_call" | custom-call | flops 17179869184 | bytes 41943040 | tf_op jit(solution)/shard_map/pallas_call | solution.py:300
  278.7 0.0 copy-start
  278.7 1.6 copy-done
  280.3 0.0 copy-start.1
  280.3 1.6 copy-done.1
  281.8 16.1 %shard_map.131 = (bf16[2,1024,2048]{2,1,0:T(8,128)(2,1)}, f32[1,2048]{1,0:T(1,128)}, bf16[2,2048,1024]{2,1,0:T(8,128)(2,1)}) custom-call(bf16[2,512,1024]{2,1,0:T(8,128)(2,1)S(1)} %copy-done, bf16[2,512,1024]{2,1,0:T(8,128)(2,1)S(1)} %copy-done.1, bf16[512,2048]{1,0:T(8,128)(2,1)} %get-tuple-element.12.feat, bf16[512,2048]{1,0:T(8,128)(2,1)} %get-tuple-element.13.dpre, ...), custom_call_target="tpu_custom_call" | custom-call | tf_op jit(solution)/shard_map/pallas_call | solution.py:369
Async XLA Ops:
  278.7 1.6 copy-start
  280.3 1.6 copy-start.1
